TPU v7x, 32 devices: a whole 2x2x4 slice. The times are simulated.
32 devices in a mesh: parts: 2 (over y), tm: 16 (over z, x, core).
Axes of the slice: x: 2, y: 2, z: 4, core: 2. Of those that a mesh axis runs over, the one named last changes fastest.
Arguments:
- frames: bfloat16 [2048, 2048], P('tm', 'parts'), parts along dimension 1, may hold values from -6 to 6
- levels: int32 [2048], P(('parts', 'tm')), parts along dimension 0, may hold values from 0 to 15
- initial_state: float32 [256], P('parts'), parts along dimension 0, may hold values from -6 to 6
- transitions: float32 [16, 128, 128], replicated, may hold values from -1 to 1
- gain: bfloat16 [128, 128], replicated, may hold values from -1 to 1
- pixel_mode: int32 [2048], replicated, may hold values from 0 to 127
- pixel_weight: bfloat16 [2048], replicated, may hold values from 0.099609375 to 0.5
Outputs:
- estimates: float32 [2048, 128], P(('parts', 'tm')), parts along dimension 0
There are 2 independent parts, one for each index of `parts`. A program takes and returns all parts, laid end to end along the dimension named above; an argument that names none is the same for every part. Nothing has to cross between parts.
All inputs are finite; a program needn't handle non-finite values.
Results may differ from a plain program's by a relative error of at most 0.0026.
Values may be sent and summed in bfloat16 or wider, within the bound.
No kernel may reach another device: no remote copies, remote signals or barrier semaphores. Data moves between devices by JAX's collectives and lax.ppermute only.
A program may use at most 128 MiB of HBM per device.

v0:
```python
import functools

import jax
import jax.numpy as jnp
from jax import lax
from jax.experimental import pallas as pl
from jax.experimental.pallas import tpu as pltpu
from jax.sharding import PartitionSpec as P

F32 = jnp.float32
BF16 = jnp.bfloat16
MIB = 1 << 20
NT = (((1,), (1,)), ((), ()))
VMEM = pl.BlockSpec(memory_space=pltpu.VMEM)
SMEM = pl.BlockSpec(memory_space=pltpu.SMEM)


def params(mib):
    return pltpu.CompilerParams(vmem_limit_bytes=mib * MIB)


def split3(x):
    high = x.astype(BF16)
    rest = x - high.astype(F32)
    mid = rest.astype(BF16)
    low = (rest - mid.astype(F32)).astype(BF16)
    return high, mid, low


def pair(x):
    high = x.astype(BF16)
    mid = (x - high.astype(F32)).astype(BF16)
    return jnp.concatenate([high, mid], axis=1)


def mm(left, right):
    lh, lm, ll = left
    rh, rm, rl = right
    wide = jnp.concatenate([rh, rm], axis=1)
    main = jnp.dot(
        jnp.concatenate([lh, lm], axis=1),
        jnp.concatenate([wide, wide], axis=0),
        preferred_element_type=F32,
    )
    rest = jnp.dot(
        jnp.concatenate([lh, ll], axis=1),
        jnp.concatenate([rl, rh], axis=0),
        preferred_element_type=F32,
    )
    n = rh.shape[1]
    return main[:, :n] + (main[:, n:] + rest)


def vm(vec, mat):
    high = vec.astype(BF16).astype(F32)
    rows = jnp.concatenate([high, vec - high], axis=0).astype(BF16)
    out = jnp.dot(rows, mat, preferred_element_type=F32)
    n = vec.shape[1]
    out = out[:, :n] + out[:, n:]
    return out[:8] + out[8:]


def transpose_kernel(frames_ref, out_ref):
    out_ref[...] = frames_ref[...].T


def tree_kernel(steps, levels_ref, trans_ref, left_ref, right_ref, table_ref, total_ref, tlow_ref, llow_ref, rlow_ref):
    kinds, n, _ = trans_ref.shape

    def prepare(k, c):
        high, mid, low = split3(trans_ref[k].T)
        table_ref[k] = jnp.concatenate([high, mid], axis=1)
        tlow_ref[k] = low
        return c

    lax.fori_loop(0, kinds, prepare, 0)

    def load(hm_ref, low_ref, k):
        hm = hm_ref[k]
        return hm[:, :n], hm[:, n:], low_ref[k]

    def store(hm_ref, low_ref, k, x):
        high, mid, low = split3(x)
        hm_ref[k] = jnp.concatenate([high, mid], axis=1)
        low_ref[k] = low

    def first(t):
        return mm(load(table_ref, tlow_ref, levels_ref[t]), load(table_ref, tlow_ref, levels_ref[t + 1]))

    def node(k):
        return mm(load(left_ref, llow_ref, k), load(right_ref, rlow_ref, k))

    base = steps // 4

    def first_pairs(ks):
        made = [(first(4 * k), first(4 * k + 2)) for k in ks]
        for k, (a, b) in zip(ks, made):
            store(left_ref, llow_ref, k, a)
            store(right_ref, rlow_ref, k, b)

    def later_pairs(ks):
        made = [(node(2 * (k - base)), node(2 * (k - base) + 1)) for k in ks]
        for k, (a, b) in zip(ks, made):
            store(left_ref, llow_ref, k, a)
            store(right_ref, rlow_ref, k, b)

    def loop(fn, start, count):
        def body(i, c):
            fn([start + 2 * i, start + 2 * i + 1])
            return c

        lax.fori_loop(0, count // 2, body, 0)

    loop(first_pairs, 0, base)
    count, start = base // 2, base
    while count >= 2:
        loop(later_pairs, start, count)
        start += count
        count //= 2
    later_pairs([start])
    total_ref[...] = node(start)


def group_kernel(size, pos_ref, *refs):
    maps = refs[:size]
    prefix_ref, whole_ref, all_ref = refs[size:]
    n = whole_ref.shape[0]
    member = pos_ref[0] % size
    for r in range(size):
        all_ref[(member + r) % size] = maps[r][...]
    prefix_ref[...] = pair((jax.lax.broadcasted_iota(jnp.int32, (n, n), 0) == jax.lax.broadcasted_iota(jnp.int32, (n, n), 1)).astype(F32))
    run = all_ref[0]
    for q in range(1, size):
        @pl.when(member == q)
        def _(run=run):
            prefix_ref[...] = pair(run)
        run = mm(split3(run), split3(all_ref[q]))
    whole_ref[...] = run


def row(ref, t):
    return jnp.broadcast_to(ref[pl.ds(t, 1), :], (8, ref.shape[1]))


def local_kernel(size, groups, pos_ref, levels_ref, x_ref, mode_ref, weight_ref, gain_ref, init_ref, table_ref, right_ref, total_ref, *refs):
    members = refs[: size - 1]
    wholes = refs[size - 1 : size - 1 + groups - 2]
    lefts_ref, sent_ref, drive_ref = refs[size - 1 + groups - 2 :]
    segments, steps, width = x_ref.shape
    n = gain_ref.shape[0]
    channel = lax.broadcasted_iota(jnp.int32, (n, width), 0)
    measured = jnp.zeros((steps, n), F32)
    for k in range(segments):
        weight = jnp.broadcast_to(weight_ref[pl.ds(k, 1), :].astype(F32), (n, width))
        projector = jnp.where(mode_ref[pl.ds(k, 1), :] == channel, weight, 0.0).astype(BF16)
        measured += lax.dot_general(x_ref[k], projector, NT, preferred_element_type=F32)
    drive_ref[...] = lax.dot_general(measured.astype(BF16), gain_ref[...], NT, preferred_element_type=F32)

    states = [row(drive_ref, t) for t in range(steps)]
    at, offset = 0, 0
    for level in range(steps.bit_length() - 1):
        later = []
        for i in range(len(states) // 2):
            mat = table_ref[levels_ref[2 * i + 1]] if level == 0 else right_ref[offset + i]
            lefts_ref[pl.ds(at + i, 1), :] = states[2 * i][:1]
            later.append(vm(states[2 * i], mat) + states[2 * i + 1])
        at += len(later)
        if level > 0:
            offset += len(later)
        states = later
    total = states[0]
    lefts_ref[pl.ds(at, 1), :] = total[:1]

    position = pos_ref[0]
    first = jnp.where(position == 0, row(init_ref, 0), 0.0)
    carried = total + vm(first, pair(total_ref[...]))
    sent_ref[...] = jnp.zeros_like(sent_ref)
    member = position % size
    group = position // size
    for r in range(1, size):
        @pl.when(member + r < size)
        def _(carried=carried, r=r):
            sent_ref[position + r] = carried[:1]
        carried = jnp.where(member + r < size, vm(carried, pair(members[r - 1][...])), carried)
    for r in range(1, groups):
        @pl.when(group + r < groups)
        def _(carried=carried, r=r):
            for q in range(size):
                sent_ref[(group + r) * size + q] = carried[:1]
        if r < groups - 1:
            carried = vm(carried, pair(wholes[r - 1][...]))


def final_kernel(size, pos_ref, levels_ref, got_ref, init_ref, prefix_ref, table_ref, left_ref, total_ref, lefts_ref, out_ref):
    steps, n = lefts_ref.shape
    position = pos_ref[0]
    start = position // size * size
    sender = lax.broadcasted_iota(jnp.int32, got_ref.shape, 0)
    got = got_ref[...]
    before = jnp.sum(jnp.where(sender < start, got, 0.0), axis=0)
    beside = jnp.sum(jnp.where(sender >= start, got, 0.0), axis=0)
    before = jnp.broadcast_to(before, (8, n))
    beside = jnp.broadcast_to(beside, (8, n))
    first = jnp.where(position == 0, row(init_ref, 0), 0.0)
    state = vm(before, prefix_ref[...]) + beside + first
    levels = steps.bit_length() - 1
    starts = [state]
    sizes = [steps >> (level + 1) for level in range(levels)]
    for level in reversed(range(levels)):
        at, offset = sum(sizes[:level]), sum(sizes[1:level])
        later = []
        for i, x in enumerate(starts):
            mat = table_ref[levels_ref[2 * i]] if level == 0 else left_ref[offset + i]
            later += [x, vm(x, mat) + row(lefts_ref, at + i)]
        starts = later
    for t in range(1, steps):
        out_ref[pl.ds(t - 1, 1), :] = starts[t][:1]
    out_ref[pl.ds(steps - 1, 1), :] = (vm(state, pair(total_ref[...])) + row(lefts_ref, steps - 1))[:1]


def shards(count, frames, levels, initial_state, transitions, gain, pixel_mode, pixel_weight):
    n = gain.shape[0]
    pixels, length = frames.shape
    steps = length // count
    size = 1
    while count % (2 * size) == 0 and 4 * size * size <= count:
        size *= 2
    groups = count // size
    position = lax.axis_index("tm").astype(jnp.int32)[None]
    initial_state = initial_state[None]
    pairs = steps // 2 - 1

    if pixels % 128 == 0:
        turned = pl.pallas_call(
            transpose_kernel,
            out_shape=jax.ShapeDtypeStruct((length, pixels), BF16),
            in_specs=[VMEM],
            out_specs=VMEM,
            compiler_params=params(16),
            name="turn_frames",
        )(frames).reshape(count, steps, pixels)
        x = lax.all_to_all(turned, "tm", split_axis=0, concat_axis=0, tiled=True)
    else:
        x = lax.all_to_all(frames, "tm", split_axis=1, concat_axis=0, tiled=True).T[None]
    mode = pixel_mode.reshape(x.shape[0], x.shape[2])
    weight = pixel_weight.reshape(x.shape[0], x.shape[2])

    left, right, table, total = pl.pallas_call(
        functools.partial(tree_kernel, steps),
        out_shape=[
            jax.ShapeDtypeStruct((pairs, n, 2 * n), BF16),
            jax.ShapeDtypeStruct((pairs, n, 2 * n), BF16),
            jax.ShapeDtypeStruct((transitions.shape[0], n, 2 * n), BF16),
            jax.ShapeDtypeStruct((n, n), F32),
        ],
        in_specs=[SMEM, VMEM],
        out_specs=[VMEM] * 4,
        scratch_shapes=[
            pltpu.VMEM((transitions.shape[0], n, n), BF16),
            pltpu.VMEM((pairs, n, n), BF16),
            pltpu.VMEM((pairs, n, n), BF16),
        ],
        compiler_params=params(32),
        name="tree_of_maps",
    )(levels, transitions)

    members = [
        lax.ppermute(total, "tm", [(j // size * size + (j + r) % size, j) for j in range(count)])
        for r in range(1, size)
    ]
    prefix, whole = pl.pallas_call(
        functools.partial(group_kernel, size),
        out_shape=[jax.ShapeDtypeStruct((n, 2 * n), BF16), jax.ShapeDtypeStruct((n, n), F32)],
        in_specs=[SMEM] + [VMEM] * size,
        out_specs=[VMEM] * 2,
        scratch_shapes=[pltpu.VMEM((size, n, n), F32)],
        compiler_params=params(16),
        name="group_maps",
    )(position, total, *members)
    wholes = [
        lax.ppermute(whole, "tm", [(j + r * size, j) for j in range(count - r * size)])
        for r in range(1, groups - 1)
    ]

    lefts, sent = pl.pallas_call(
        functools.partial(local_kernel, size, groups),
        out_shape=[jax.ShapeDtypeStruct((steps, n), F32), jax.ShapeDtypeStruct((count, 1, n), F32)],
        in_specs=[SMEM, SMEM] + [VMEM] * (8 + size - 1 + groups - 2),
        out_specs=[VMEM] * 2,
        scratch_shapes=[pltpu.VMEM((steps, n), F32)],
        compiler_params=params(32),
        name="local_states",
    )(position, levels, x, mode, weight, gain, initial_state, table, right, total, *members, *wholes)
    got = lax.all_to_all(sent, "tm", split_axis=0, concat_axis=0, tiled=True)
    return pl.pallas_call(
        functools.partial(final_kernel, size),
        out_shape=jax.ShapeDtypeStruct((steps, n), F32),
        in_specs=[SMEM, SMEM] + [VMEM] * 7,
        out_specs=VMEM,
        compiler_params=params(32),
        name="estimates",
    )(position, levels, got, initial_state, prefix, table, left, total, lefts)


def solution(mesh):
    in_specs = (P("tm", "parts"), P(("parts", "tm")), P("parts"), P(), P(), P(), P())
    out_specs = P(("parts", "tm"), None)
    return jax.shard_map(
        functools.partial(shards, mesh.shape["tm"]),
        mesh=mesh,
        in_specs=in_specs,
        out_specs=out_specs,
        check_vma=False,
    )
```

profile of v0, /device:TPU:0, one launch (start us, length us, event | category | flops | bytes accessed | tf_op | source)
XLA Modules:
  0.0 57.7 jit_solution(5600577006884504479)
XLA Ops:
  0.0 0.0 copy-start.3
  0.0 0.9 %copy-done.3 = bf16[128,1024]{1,0:T(8,128)(2,1)S(1)} copy-done((bf16[128,1024]{1,0:T(8,128)(2,1)S(1)}, bf16[128,1024]{1,0:T(8,128)(2,1)}, u32[]{:S(2)}) %copy-start.3) | copy-done | bytes 262168
  1.0 0.0 copy-start.11
  1.0 0.0 copy-start.13
  1.0 0.0 copy-start.14
  1.0 0.8 %turn_frames.1 = bf16[1024,128]{1,0:T(8,128)(2,1)} custom-call(bf16[128,1024]{1,0:T(8,128)(2,1)S(1)} %copy-done.3), custom_call_target="tpu_custom_call" | custom-call | tf_op jit(solution)/shard_map/turn_frames/pallas_call | solution.py:234
  1.8 7.4 %all-to-all-start = ((bf16[16,64,128]{2,1,0:T(8,128)(2,1)}), bf16[16,64,128]{2,1,0:T(8,128)(2,1)S(1)}, u32[]{:S(2)}, u32[]{:S(2)}) async-start(bf16[16,64,128]{2,1,0:T(8,128)(2,1)} %bitcast.1), calls=%async_computation | async-start | bytes 524288 | tf_op jit(solution)/shard_map/all_to_all | solution.py:242
  9.1 0.0 copy-start.2
  9.2 1.2 %copy-done.2 = f32[16,128,128]{2,1,0:T(8,128)S(1)} copy-done((f32[16,128,128]{2,1,0:T(8,128)S(1)}, f32[16,128,128]{2,1,0:T(8,128)}, u32[]{:S(2)}) %copy-start.2) | copy-done | bytes 1048600
  10.4 0.0 copy-start.12
  10.4 0.7 %copy-done.12 = s32[64]{0:T(128)S(1)} copy-done((s32[64]{0:T(128)S(1)}, s32[64]{0:T(128)}, u32[]{:S(2)}) %copy-start.12) | copy-done | bytes 280
  11.0 7.2 %tree_of_maps.1 = (bf16[31,128,256]{2,1,0:T(8,128)(2,1)S(1)}, bf16[31,128,256]{2,1,0:T(8,128)(2,1)S(1)}, bf16[16,128,256]{2,1,0:T(8,128)(2,1)S(1)}, f32[128,128]{1,0:T(8,128)S(1)}) custom-call(s32[64]{0:T(128)S(1)} %copy-done.12, f32[16,128,128]{2,1,0:T(8,128)S(1)} %copy-done.2), custom_call_target="tpu_custom_call" | custom-call | tf_op jit(solution)/shard_map/tree_of_maps/pallas_call | solution.py:248
  18.3 0.0 copy-start
  18.3 1.3 %copy-done = bf16[31,128,256]{2,1,0:T(8,128)(2,1)} copy-done((bf16[31,128,256]{2,1,0:T(8,128)(2,1)}, bf16[31,128,256]{2,1,0:T(8,128)(2,1)S(1)}, u32[]{:S(2)}) %copy-start) | copy-done | bytes 2031640
  19.6 0.4 collective-permute-start.2
  20.0 1.7 %collective-permute-start.1 = (f32[128,128]{1,0:T(8,128)S(1)}, f32[128,128]{1,0:T(8,128)S(1)}, u32[]{:S(2)}, u32[]{:S(2)}) collective-permute-start(f32[128,128]{1,0:T(8,128)S(1)} %get-tuple-element.15.refs_0_.total_ref), channel_id=1, source_target_pairs={{2,0},{3,1},{0,2},{1,3},{6,4},{7,5},{4,6},{5,7},{10,8},{11,9},{8,1... | collective-permute-start | bytes 196616 | tf_op jit(solution)/shard_map/ppermute | solution.py:268
  21.6 1.3 %collective-permute-start = (f32[128,128]{1,0:T(8,128)S(1)}, f32[128,128]{1,0:T(8,128)}, u32[]{:S(2)}, u32[]{:S(2)}) collective-permute-start(f32[128,128]{1,0:T(8,128)S(1)} %get-tuple-element.15.refs_0_.total_ref), channel_id=1, source_target_pairs={{1,0},{2,1},{3,2},{0,3},{5,4},{6,5},{7,6},{4,7},{9,8},{10,9},{11,1... | collective-permute-start | bytes 196616 | tf_op jit(solution)/shard_map/ppermute | solution.py:268
  22.9 0.3 collective-permute-done.2.refs_3_.refs_2_
  23.3 1.1 %collective-permute-done.1.refs_2_.refs_1_ = f32[128,128]{1,0:T(8,128)S(1)} collective-permute-done((f32[128,128]{1,0:T(8,128)S(1)}, f32[128,128]{1,0:T(8,128)S(1)}, u32[]{:S(2)}, u32[]{:S(2)}) %collective-permute-start.1) | collective-permute-done | bytes 65568 | tf_op jit(solution)/shard_map/ppermute | solution.py:268
  24.3 0.5 collective-permute-done.refs_1_.refs_0_
  24.9 1.4 %group_maps.1 = (bf16[128,256]{1,0:T(8,128)(2,1)S(1)}, f32[128,128]{1,0:T(8,128)S(1)}) custom-call(s32[1]{0:T(128)} %bitcast.pos_ref, f32[128,128]{1,0:T(8,128)S(1)} %get-tuple-element.15.refs_0_.total_ref, f32[128,128]{1,0:T(8,128)} %collective-permute-done.refs_1_.refs_0_, f32[128,128]{1,0:T(8,128)S(1)} %collective-permute-done.1.refs_2_.refs_1_, ...), custom_call_target="tpu_custom_call" | custom-call | tf_op jit(solution)/shard_map/group_maps/pallas_call | solution.py:271
  26.3 0.0 copy-start.8
  26.3 0.6 %copy-done.8 = bf16[128,256]{1,0:T(8,128)(2,1)} copy-done((bf16[128,256]{1,0:T(8,128)(2,1)}, bf16[128,256]{1,0:T(8,128)(2,1)S(1)}, u32[]{:S(2)}) %copy-start.8) | copy-done | bytes 65560
  26.9 1.3 %collective-permute-start.4 = (f32[128,128]{1,0:T(8,128)S(1)}, f32[128,128]{1,0:T(8,128)S(1)}, u32[]{:S(2)}, u32[]{:S(2)}) collective-permute-start(f32[128,128]{1,0:T(8,128)S(1)} %get-tuple-element.16), channel_id=1, source_target_pairs={{8,0},{9,1},{10,2},{11,3},{12,4},{13,5},{14,6},{15,7},{24,16},{25,... | collective-permute-start | bytes 196616 | tf_op jit(solution)/shard_map/ppermute | solution.py:281
  28.2 1.3 %collective-permute-start.3 = (f32[128,128]{1,0:T(8,128)S(1)}, f32[128,128]{1,0:T(8,128)S(1)}, u32[]{:S(2)}, u32[]{:S(2)}) collective-permute-start(f32[128,128]{1,0:T(8,128)S(1)} %get-tuple-element.16), channel_id=1, source_target_pairs={{4,0},{5,1},{6,2},{7,3},{8,4},{9,5},{10,6},{11,7},{12,8},{13,9},{1... | collective-permute-start | bytes 196616 | tf_op jit(solution)/shard_map/ppermute | solution.py:281
  29.5 6.4 %collective-permute-done.4.refs_4_ = f32[128,128]{1,0:T(8,128)S(1)} collective-permute-done((f32[128,128]{1,0:T(8,128)S(1)}, f32[128,128]{1,0:T(8,128)S(1)}, u32[]{:S(2)}, u32[]{:S(2)}) %collective-permute-start.4) | collective-permute-done | bytes 65568 | tf_op jit(solution)/shard_map/ppermute | solution.py:281
  36.0 0.0 copy-start.4
  36.0 0.6 %copy-done.4 = f32[128,128]{1,0:T(8,128)} copy-done((f32[128,128]{1,0:T(8,128)}, f32[128,128]{1,0:T(8,128)S(1)}, u32[]{:S(2)}) %copy-start.4) | copy-done | bytes 65560
  36.6 0.0 collective-permute-done.3.refs_3_
  36.6 0.0 copy-start.6
  36.6 0.6 %copy-done.6 = f32[128,128]{1,0:T(8,128)} copy-done((f32[128,128]{1,0:T(8,128)}, f32[128,128]{1,0:T(8,128)S(1)}, u32[]{:S(2)}) %copy-start.6) | copy-done | bytes 65560
  37.2 0.0 all-to-all-done.x_ref
  37.2 0.0 copy-done.11
  37.2 0.0 copy-done.13
  37.2 0.0 copy-done.14
  37.2 0.0 copy-start.1
  37.2 1.6 %copy-done.1 = bf16[31,128,256]{2,1,0:T(8,128)(2,1)S(1)} copy-done((bf16[31,128,256]{2,1,0:T(8,128)(2,1)S(1)}, bf16[31,128,256]{2,1,0:T(8,128)(2,1)}, u32[]{:S(2)}) %copy-start.1) | copy-done | bytes 2031640
  38.8 0.0 copy-start.5
  38.8 0.8 %copy-done.5 = f32[128,128]{1,0:T(8,128)S(1)} copy-done((f32[128,128]{1,0:T(8,128)S(1)}, f32[128,128]{1,0:T(8,128)}, u32[]{:S(2)}) %copy-start.5) | copy-done | bytes 65560
  39.6 0.0 copy-start.7
  39.6 0.8 %copy-done.7 = f32[128,128]{1,0:T(8,128)S(1)} copy-done((f32[128,128]{1,0:T(8,128)S(1)}, f32[128,128]{1,0:T(8,128)}, u32[]{:S(2)}) %copy-start.7) | copy-done | bytes 65560
  40.5 0.0 copy-start.10
  40.5 0.8 %copy-done.10 = bf16[128,128]{1,0:T(8,128)(2,1)S(1)} copy-done((bf16[128,128]{1,0:T(8,128)(2,1)S(1)}, bf16[128,128]{1,0:T(8,128)(2,1)}, u32[]{:S(2)}) %copy-start.10) | copy-done | bytes 32792
  41.2 0.0 copy-start.15
  41.2 0.7 %copy-done.15 = f32[128]{0:T(128)S(1)} copy-done((f32[128]{0:T(128)S(1)}, f32[128]{0:T(128)}, u32[]{:S(2)}) %copy-start.15) | copy-done | bytes 536
  41.9 0.0 copy-start.9
  41.9 3.5 %local_states.1 = (f32[64,128]{1,0:T(8,128)S(1)}, f32[16,1,128]{2,1,0:T(1,128)S(1)}) custom-call(s32[1]{0:T(128)} %bitcast.pos_ref, s32[64]{0:T(128)S(1)} %copy-done.13, bf16[16,64,128]{2,1,0:T(8,128)(2,1)S(1)} %all-to-all-done.x_ref, s32[16,128]{1,0:T(8,128)S(1)} %bitcast.5, bf16[16,128]{1,0:T(8,128)(2,1)S(1)} %bitcast.6, bf16[128,128]{1,0:T(8,128)(2,1)S(1)} %copy-done.10, ...), custom_call_target="tpu_custom_call" | custom-call | tf_op jit(solution)/shard_map/local_states/pallas_call | solution.py:285
  45.3 10.2 %all_to_all.10.got_ref = f32[16,1,128]{2,1,0:T(1,128)S(1)} all-to-all(f32[16,1,128]{2,1,0:T(1,128)S(1)} %get-tuple-element.17), channel_id=1, replica_groups=mesh['parts'=2,'tm'=16] {'tm'}, dimensions={0} | all-to-all | bytes 16384 | tf_op jit(solution)/shard_map/all_to_all | solution.py:294
  55.5 0.0 copy-done.9
  55.5 2.2 %estimates.1 = f32[64,128]{1,0:T(8,128)} custom-call(s32[1]{0:T(128)} %bitcast.pos_ref, s32[64]{0:T(128)S(1)} %copy-done.13, f32[16,1,128]{2,1,0:T(1,128)S(1)} %all_to_all.10.got_ref, f32[1,128]{1,0:T(1,128)S(1)} %bitcast.8, bf16[128,256]{1,0:T(8,128)(2,1)S(1)} %copy-done.9, bf16[16,128,256]{2,1,0:T(8,128)(2,1)S(1)} %get-tuple-element.13.table_ref, ...), custom_call_target="tpu_custom_call" | custom-call | tf_op jit(solution)/shard_map/estimates/pallas_call | solution.py:295
Async XLA Ops:
  0.0 0.9 %copy-start.3 = (bf16[128,1024]{1,0:T(8,128)(2,1)S(1)}, bf16[128,1024]{1,0:T(8,128)(2,1)}, u32[]{:S(2)}) copy-start(bf16[128,1024]{1,0:T(8,128)(2,1)} %frames_ref.1) | copy-start | bytes 786436
  1.0 36.3 %copy-start.11 = (s32[2048]{0:T(1024)S(1)}, s32[2048]{0:T(1024)}, u32[]{:S(2)}) copy-start(s32[2048]{0:T(1024)} %param.12) | copy-start | bytes 24580
  1.0 36.3 %copy-start.13 = (s32[64]{0:T(128)S(1)}, s32[64]{0:T(128)}, u32[]{:S(2)}) copy-start(s32[64]{0:T(128)} %levels_ref.5) | copy-start | bytes 772
  1.0 36.3 %copy-start.14 = (bf16[2048]{0:T(1024)(128)(2,1)S(1)}, bf16[2048]{0:T(1024)(128)(2,1)}, u32[]{:S(2)}) copy-start(bf16[2048]{0:T(1024)(128)(2,1)} %param.13) | copy-start | bytes 12292
  1.8 35.4 %all-to-all-start = ((bf16[16,64,128]{2,1,0:T(8,128)(2,1)}), bf16[16,64,128]{2,1,0:T(8,128)(2,1)S(1)}, u32[]{:S(2)}, u32[]{:S(2)}) async-start(bf16[16,64,128]{2,1,0:T(8,128)(2,1)} %bitcast.1), calls=%async_computation | async-start | bytes 524288 | tf_op jit(solution)/shard_map/all_to_all | solution.py:242
  9.1 1.2 %copy-start.2 = (f32[16,128,128]{2,1,0:T(8,128)S(1)}, f32[16,128,128]{2,1,0:T(8,128)}, u32[]{:S(2)}) copy-start(f32[16,128,128]{2,1,0:T(8,128)} %trans_ref.1) | copy-start | bytes 3145732
  10.4 0.7 %copy-start.12 = (s32[64]{0:T(128)S(1)}, s32[64]{0:T(128)}, u32[]{:S(2)}) copy-start(s32[64]{0:T(128)} %levels_ref.5) | copy-start | bytes 772
  18.3 1.3 %copy-start = (bf16[31,128,256]{2,1,0:T(8,128)(2,1)}, bf16[31,128,256]{2,1,0:T(8,128)(2,1)S(1)}, u32[]{:S(2)}) copy-start(bf16[31,128,256]{2,1,0:T(8,128)(2,1)S(1)} %get-tuple-element.14.right_ref) | copy-start | bytes 6094852
  19.6 3.7 %collective-permute-start.2 = (f32[128,128]{1,0:T(8,128)S(1)}, f32[128,128]{1,0:T(8,128)S(1)}, u32[]{:S(2)}, u32[]{:S(2)}) collective-permute-start(f32[128,128]{1,0:T(8,128)S(1)} %get-tuple-element.15.refs_0_.total_ref), channel_id=1, source_target_pairs={{3,0},{0,1},{1,2},{2,3},{7,4},{4,5},{5,6},{6,7},{11,8},{8,9},{9,10... | collective-permute-start | bytes 196616 | tf_op jit(solution)/shard_map/ppermute | solution.py:268
  20.0 4.4 %collective-permute-start.1 = (f32[128,128]{1,0:T(8,128)S(1)}, f32[128,128]{1,0:T(8,128)S(1)}, u32[]{:S(2)}, u32[]{:S(2)}) collective-permute-start(f32[128,128]{1,0:T(8,128)S(1)} %get-tuple-element.15.refs_0_.total_ref), channel_id=1, source_target_pairs={{2,0},{3,1},{0,2},{1,3},{6,4},{7,5},{4,6},{5,7},{10,8},{11,9},{8,1... | collective-permute-start | bytes 196616 | tf_op jit(solution)/shard_map/ppermute | solution.py:268
  21.6 3.2 %collective-permute-start = (f32[128,128]{1,0:T(8,128)S(1)}, f32[128,128]{1,0:T(8,128)}, u32[]{:S(2)}, u32[]{:S(2)}) collective-permute-start(f32[128,128]{1,0:T(8,128)S(1)} %get-tuple-element.15.refs_0_.total_ref), channel_id=1, source_target_pairs={{1,0},{2,1},{3,2},{0,3},{5,4},{6,5},{7,6},{4,7},{9,8},{10,9},{11,1... | collective-permute-start | bytes 196616 | tf_op jit(solution)/shard_map/ppermute | solution.py:268
  26.3 0.6 %copy-start.8 = (bf16[128,256]{1,0:T(8,128)(2,1)}, bf16[128,256]{1,0:T(8,128)(2,1)S(1)}, u32[]{:S(2)}) copy-start(bf16[128,256]{1,0:T(8,128)(2,1)S(1)} %get-tuple-element.18.prefix_ref) | copy-start | bytes 196612
  26.9 9.0 %collective-permute-start.4 = (f32[128,128]{1,0:T(8,128)S(1)}, f32[128,128]{1,0:T(8,128)S(1)}, u32[]{:S(2)}, u32[]{:S(2)}) collective-permute-start(f32[128,128]{1,0:T(8,128)S(1)} %get-tuple-element.16), channel_id=1, source_target_pairs={{8,0},{9,1},{10,2},{11,3},{12,4},{13,5},{14,6},{15,7},{24,16},{25,... | collective-permute-start | bytes 196616 | tf_op jit(solution)/shard_map/ppermute | solution.py:281
  28.2 8.4 %collective-permute-start.3 = (f32[128,128]{1,0:T(8,128)S(1)}, f32[128,128]{1,0:T(8,128)S(1)}, u32[]{:S(2)}, u32[]{:S(2)}) collective-permute-start(f32[128,128]{1,0:T(8,128)S(1)} %get-tuple-element.16), channel_id=1, source_target_pairs={{4,0},{5,1},{6,2},{7,3},{8,4},{9,5},{10,6},{11,7},{12,8},{13,9},{1... | collective-permute-start | bytes 196616 | tf_op jit(solution)/shard_map/ppermute | solution.py:281
  36.0 0.6 %copy-start.4 = (f32[128,128]{1,0:T(8,128)}, f32[128,128]{1,0:T(8,128)S(1)}, u32[]{:S(2)}) copy-start(f32[128,128]{1,0:T(8,128)S(1)} %collective-permute-done.4.refs_4_) | copy-start | bytes 196612
  36.6 0.6 %copy-start.6 = (f32[128,128]{1,0:T(8,128)}, f32[128,128]{1,0:T(8,128)S(1)}, u32[]{:S(2)}) copy-start(f32[128,128]{1,0:T(8,128)S(1)} %collective-permute-done.3.refs_3_) | copy-start | bytes 196612
  37.2 1.6 %copy-start.1 = (bf16[31,128,256]{2,1,0:T(8,128)(2,1)S(1)}, bf16[31,128,256]{2,1,0:T(8,128)(2,1)}, u32[]{:S(2)}) copy-start(bf16[31,128,256]{2,1,0:T(8,128)(2,1)} %copy-done) | copy-start | bytes 6094852
  38.8 0.8 %copy-start.5 = (f32[128,128]{1,0:T(8,128)S(1)}, f32[128,128]{1,0:T(8,128)}, u32[]{:S(2)}) copy-start(f32[128,128]{1,0:T(8,128)} %copy-done.4) | copy-start | bytes 196612
  39.6 0.8 %copy-start.7 = (f32[128,128]{1,0:T(8,128)S(1)}, f32[128,128]{1,0:T(8,128)}, u32[]{:S(2)}) copy-start(f32[128,128]{1,0:T(8,128)} %copy-done.6) | copy-start | bytes 196612
  40.5 0.8 %copy-start.10 = (bf16[128,128]{1,0:T(8,128)(2,1)S(1)}, bf16[128,128]{1,0:T(8,128)(2,1)}, u32[]{:S(2)}) copy-start(bf16[128,128]{1,0:T(8,128)(2,1)} %gain_ref.1) | copy-start | bytes 98308
  41.2 0.7 %copy-start.15 = (f32[128]{0:T(128)S(1)}, f32[128]{0:T(128)}, u32[]{:S(2)}) copy-start(f32[128]{0:T(128)} %param.9) | copy-start | bytes 1540
  41.9 13.6 %copy-start.9 = (bf16[128,256]{1,0:T(8,128)(2,1)S(1)}, bf16[128,256]{1,0:T(8,128)(2,1)}, u32[]{:S(2)}) copy-start(bf16[128,256]{1,0:T(8,128)(2,1)} %copy-done.8) | copy-start | bytes 196612
where the time goes:
time: 58.4 us; the launch traced here: 57.7 us
  Pallas kernels  15.2 us (26%)
  starting transfers between devices  13.3 us (23%)
  local copies, waits for them, and re-layouts  10.7 us (18%)
  blocking collectives  10.2 us (17%)
  waiting for transfers between devices  8.35 us (14%)
    unnamed x32, local copies, waits for them, and re-layouts  10.7 us
    all_to_all x1, blocking collectives, shards(): got = lax.all_to_all(sent, 'tm', split_axis=0, concat_axis=0, tiled=True)  10.2 us
    all_to_all x1, starting transfers between devices, shards(): x = lax.all_to_all(turned, 'tm', split_axis=0, concat_axis=0, tiled=True)  7.36 us
    pallas_call x1, Pallas kernels, shards(): pl.pallas_call(functools.partial(tree_kernel, steps), out_shape=[jax.Shap...  7.22 us
    ppermute x2, waiting for transfers between devices, shards(): lax.ppermute(whole, 'tm', [(j + r * size, j) for j in range(count - r * s...  6.44 us
    pallas_call x1, Pallas kernels, shards(): pl.pallas_call(functools.partial(local_kernel, size, groups), out_shape=[...  3.46 us
    ppermute x3, starting transfers between devices, shards(): lax.ppermute(total, 'tm', [(j // size * size + (j + r) % size, j) for j i...  3.38 us
    ppermute x2, starting transfers between devices, shards(): lax.ppermute(whole, 'tm', [(j + r * size, j) for j in range(count - r * s...  2.57 us
  transfers between devices with their start and end apart: 6, of which 4 were waited for; matrix products, arithmetic and copies ran while one was open for 0% of the time, Pallas kernels for 15%

commit v1 on v0

--- a/solution.py
+++ b/solution.py
@@ -118,34 +118,32 @@
         start += count
         count //= 2
     later_pairs([start])
-    total_ref[...] = node(start)
-
-
-def group_kernel(size, pos_ref, *refs):
-    maps = refs[:size]
-    prefix_ref, whole_ref, all_ref = refs[size:]
-    n = whole_ref.shape[0]
+    total = node(start)
+    for r in range(total_ref.shape[0]):
+        total_ref[r] = total
+
+
+def group_kernel(pos_ref, maps_ref, prefix_ref, whole_ref):
+    size, n, _ = maps_ref.shape
     member = pos_ref[0] % size
-    for r in range(size):
-        all_ref[(member + r) % size] = maps[r][...]
-    prefix_ref[...] = pair((jax.lax.broadcasted_iota(jnp.int32, (n, n), 0) == jax.lax.broadcasted_iota(jnp.int32, (n, n), 1)).astype(F32))
-    run = all_ref[0]
+    rows, cols = (lax.broadcasted_iota(jnp.int32, (n, n), d) for d in (0, 1))
+    prefix_ref[...] = pair((rows == cols).astype(F32))
+    run = maps_ref[0]
     for q in range(1, size):
         @pl.when(member == q)
         def _(run=run):
             prefix_ref[...] = pair(run)
-        run = mm(split3(run), split3(all_ref[q]))
-    whole_ref[...] = run
+        run = mm(split3(run), split3(maps_ref[q]))
+    for r in range(whole_ref.shape[0]):
+        whole_ref[r] = run
 
 
 def row(ref, t):
     return jnp.broadcast_to(ref[pl.ds(t, 1), :], (8, ref.shape[1]))
 
 
-def local_kernel(size, groups, pos_ref, levels_ref, x_ref, mode_ref, weight_ref, gain_ref, init_ref, table_ref, right_ref, total_ref, *refs):
-    members = refs[: size - 1]
-    wholes = refs[size - 1 : size - 1 + groups - 2]
-    lefts_ref, sent_ref, drive_ref = refs[size - 1 + groups - 2 :]
+def local_kernel(pos_ref, levels_ref, x_ref, mode_ref, weight_ref, gain_ref, init_ref, table_ref, right_ref, total_ref, members_ref, wholes_ref, lefts_ref, sent_ref, drive_ref):
+    size, groups = members_ref.shape[0], wholes_ref.shape[0]
     segments, steps, width = x_ref.shape
     n = gain_ref.shape[0]
     channel = lax.broadcasted_iota(jnp.int32, (n, width), 0)
@@ -173,22 +171,22 @@
 
     position = pos_ref[0]
     first = jnp.where(position == 0, row(init_ref, 0), 0.0)
-    carried = total + vm(first, pair(total_ref[...]))
+    carried = total + vm(first, pair(total_ref[0]))
     sent_ref[...] = jnp.zeros_like(sent_ref)
     member = position % size
     group = position // size
-    for r in range(1, size):
-        @pl.when(member + r < size)
-        def _(carried=carried, r=r):
-            sent_ref[position + r] = carried[:1]
-        carried = jnp.where(member + r < size, vm(carried, pair(members[r - 1][...])), carried)
-    for r in range(1, groups):
-        @pl.when(group + r < groups)
-        def _(carried=carried, r=r):
+    for q in range(1, size):
+        @pl.when(member < q)
+        def _(carried=carried, q=q):
+            sent_ref[group * size + q] = carried
+        carried = jnp.where(member < q, vm(carried, pair(members_ref[q])), carried)
+    for z in range(1, groups):
+        @pl.when(group < z)
+        def _(carried=carried, z=z):
             for q in range(size):
-                sent_ref[(group + r) * size + q] = carried[:1]
-        if r < groups - 1:
-            carried = vm(carried, pair(wholes[r - 1][...]))
+                sent_ref[z * size + q] = carried
+        if z < groups - 1:
+            carried = jnp.where(group < z, vm(carried, pair(wholes_ref[z])), carried)
 
 
 def final_kernel(size, pos_ref, levels_ref, got_ref, init_ref, prefix_ref, table_ref, left_ref, total_ref, lefts_ref, out_ref):
@@ -199,8 +197,6 @@
     got = got_ref[...]
     before = jnp.sum(jnp.where(sender < start, got, 0.0), axis=0)
     beside = jnp.sum(jnp.where(sender >= start, got, 0.0), axis=0)
-    before = jnp.broadcast_to(before, (8, n))
-    beside = jnp.broadcast_to(beside, (8, n))
     first = jnp.where(position == 0, row(init_ref, 0), 0.0)
     state = vm(before, prefix_ref[...]) + beside + first
     levels = steps.bit_length() - 1
@@ -215,7 +211,7 @@
         starts = later
     for t in range(1, steps):
         out_ref[pl.ds(t - 1, 1), :] = starts[t][:1]
-    out_ref[pl.ds(steps - 1, 1), :] = (vm(state, pair(total_ref[...])) + row(lefts_ref, steps - 1))[:1]
+    out_ref[pl.ds(steps - 1, 1), :] = (vm(state, pair(total_ref[0])) + row(lefts_ref, steps - 1))[:1]
 
 
 def shards(count, frames, levels, initial_state, transitions, gain, pixel_mode, pixel_weight):
@@ -236,7 +232,7 @@
             out_shape=jax.ShapeDtypeStruct((length, pixels), BF16),
             in_specs=[VMEM],
             out_specs=VMEM,
-            compiler_params=params(16),
+            compiler_params=params(2),
             name="turn_frames",
         )(frames).reshape(count, steps, pixels)
         x = lax.all_to_all(turned, "tm", split_axis=0, concat_axis=0, tiled=True)
@@ -251,7 +247,7 @@
             jax.ShapeDtypeStruct((pairs, n, 2 * n), BF16),
             jax.ShapeDtypeStruct((pairs, n, 2 * n), BF16),
             jax.ShapeDtypeStruct((transitions.shape[0], n, 2 * n), BF16),
-            jax.ShapeDtypeStruct((n, n), F32),
+            jax.ShapeDtypeStruct((size, n, n), F32),
         ],
         in_specs=[SMEM, VMEM],
         out_specs=[VMEM] * 4,
@@ -260,44 +256,39 @@
             pltpu.VMEM((pairs, n, n), BF16),
             pltpu.VMEM((pairs, n, n), BF16),
         ],
-        compiler_params=params(32),
+        compiler_params=params(12),
         name="tree_of_maps",
     )(levels, transitions)
 
-    members = [
-        lax.ppermute(total, "tm", [(j // size * size + (j + r) % size, j) for j in range(count)])
-        for r in range(1, size)
-    ]
+    beside = [[g * size + q for q in range(size)] for g in range(groups)]
+    across = [[g * size + q for g in range(groups)] for q in range(size)]
+    members = lax.all_to_all(total, "tm", 0, 0, axis_index_groups=beside, tiled=True)
     prefix, whole = pl.pallas_call(
-        functools.partial(group_kernel, size),
-        out_shape=[jax.ShapeDtypeStruct((n, 2 * n), BF16), jax.ShapeDtypeStruct((n, n), F32)],
-        in_specs=[SMEM] + [VMEM] * size,
+        group_kernel,
+        out_shape=[jax.ShapeDtypeStruct((n, 2 * n), BF16), jax.ShapeDtypeStruct((groups, n, n), F32)],
+        in_specs=[SMEM, VMEM],
         out_specs=[VMEM] * 2,
-        scratch_shapes=[pltpu.VMEM((size, n, n), F32)],
-        compiler_params=params(16),
+        compiler_params=params(4),
         name="group_maps",
-    )(position, total, *members)
-    wholes = [
-        lax.ppermute(whole, "tm", [(j + r * size, j) for j in range(count - r * size)])
-        for r in range(1, groups - 1)
-    ]
+    )(position, members)
+    wholes = lax.all_to_all(whole, "tm", 0, 0, axis_index_groups=across, tiled=True)
 
     lefts, sent = pl.pallas_call(
-        functools.partial(local_kernel, size, groups),
-        out_shape=[jax.ShapeDtypeStruct((steps, n), F32), jax.ShapeDtypeStruct((count, 1, n), F32)],
-        in_specs=[SMEM, SMEM] + [VMEM] * (8 + size - 1 + groups - 2),
+        local_kernel,
+        out_shape=[jax.ShapeDtypeStruct((steps, n), F32), jax.ShapeDtypeStruct((count, 8, n), F32)],
+        in_specs=[SMEM, SMEM] + [VMEM] * 10,
         out_specs=[VMEM] * 2,
         scratch_shapes=[pltpu.VMEM((steps, n), F32)],
-        compiler_params=params(32),
+        compiler_params=params(8),
         name="local_states",
-    )(position, levels, x, mode, weight, gain, initial_state, table, right, total, *members, *wholes)
+    )(position, levels, x, mode, weight, gain, initial_state, table, right, total, members, wholes)
     got = lax.all_to_all(sent, "tm", split_axis=0, concat_axis=0, tiled=True)
     return pl.pallas_call(
         functools.partial(final_kernel, size),
         out_shape=jax.ShapeDtypeStruct((steps, n), F32),
         in_specs=[SMEM, SMEM] + [VMEM] * 7,
         out_specs=VMEM,
-        compiler_params=params(32),
+        compiler_params=params(8),
         name="estimates",
     )(position, levels, got, initial_state, prefix, table, left, total, lefts)
 

time: 58.4 us -> 67.7 us (1.16)
  blocking collectives: 10.2 us -> 22.2 us
  waiting for transfers between devices: 8.35 us -> 13 us
  local copies, waits for them, and re-layouts: 10.7 us -> 7.14 us
  starting transfers between devices: 13.3 us -> 9.85 us
    all_to_all x0 -> x1, blocking collectives: none -> 12.5 us  [shards(): lax.all_to_all(whole, 'tm', 0, 0, axis_index_groups=across, tiled=True)]
    all_to_all x1, waiting for transfers between devices: 0.01 us -> 8.77 us  [shards(): x = lax.all_to_all(turned, 'tm', split_axis=0, concat_axis=0, tiled=True)]
    ppermute x5 -> x0, waiting for transfers between devices: 8.35 us -> none  [the longest x2 6.44 us: shards(): lax.ppermute(whole, 'tm', [(j + r * size, j) for j in range(count - r * s...]
    ppermute x5 -> x0, starting transfers between devices: 5.95 us -> none  [the longest x3 3.38 us: shards(): lax.ppermute(total, 'tm', [(j // size * size + (j + r) % size, j) for j i...]
    all_to_all x0 -> x1, waiting for transfers between devices: none -> 4.26 us  [shards(): lax.all_to_all(total, 'tm', 0, 0, axis_index_groups=beside, tiled=True)]
    all_to_all x0 -> x1, starting transfers between devices: none -> 4.19 us  [shards(): lax.all_to_all(total, 'tm', 0, 0, axis_index_groups=beside, tiled=True)]
    unnamed x32 -> x24, local copies, waits for them, and re-layouts: 10.7 us -> 7.14 us
    all_to_all x1, starting transfers between devices: 7.36 us -> 5.66 us  [shards(): x = lax.all_to_all(turned, 'tm', split_axis=0, concat_axis=0, tiled=True)]
  transfers between devices with their start and end apart: 6 -> 2, of which waited for: 4 -> 2; matrix products, arithmetic and copies ran while one was open for 0% -> 0% of each run, Pallas kernels for 15% -> 1%
where the time goes in v1:
time: 67.7 us; the launch traced here: 67.2 us
  blocking collectives  22.2 us (33%)
  Pallas kernels  14.9 us (22%)
  waiting for transfers between devices  13 us (19%)
  starting transfers between devices  9.85 us (15%)
  local copies, waits for them, and re-layouts  7.14 us (11%)
    all_to_all x1, blocking collectives, shards(): lax.all_to_all(whole, 'tm', 0, 0, axis_index_groups=across, tiled=True)  12.5 us
    all_to_all x1, blocking collectives, shards(): got = lax.all_to_all(sent, 'tm', split_axis=0, concat_axis=0, tiled=True)  9.64 us
    all_to_all x1, waiting for transfers between devices, shards(): x = lax.all_to_all(turned, 'tm', split_axis=0, concat_axis=0, tiled=True)  8.77 us
    pallas_call x1, Pallas kernels, shards(): pl.pallas_call(functools.partial(tree_kernel, steps), out_shape=[jax.Shap...  7.92 us
    unnamed x24, local copies, waits for them, and re-layouts  7.14 us
    all_to_all x1, starting transfers between devices, shards(): x = lax.all_to_all(turned, 'tm', split_axis=0, concat_axis=0, tiled=True)  5.66 us
    all_to_all x1, waiting for transfers between devices, shards(): lax.all_to_all(total, 'tm', 0, 0, axis_index_groups=beside, tiled=True)  4.26 us
    all_to_all x1, starting transfers between devices, shards(): lax.all_to_all(total, 'tm', 0, 0, axis_index_groups=beside, tiled=True)  4.19 us
  transfers between devices with their start and end apart: 2, of which 2 were waited for; matrix products, arithmetic and copies ran while one was open for 0% of the time, Pallas kernels for 1%

profile of v1, /device:TPU:0, one launch (start us, length us, event | category | flops | bytes accessed | tf_op | source)
XLA Modules:
  0.0 67.2 jit_solution(16976352314013920010)
XLA Ops:
  0.0 0.0 copy-start.2
  0.0 1.2 %copy-done.2 = f32[16,128,128]{2,1,0:T(8,128)S(1)} copy-done((f32[16,128,128]{2,1,0:T(8,128)S(1)}, f32[16,128,128]{2,1,0:T(8,128)}, u32[]{:S(2)}) %copy-start.2) | copy-done | bytes 1048600
  1.2 0.0 copy-start.8
  1.2 0.7 copy-done.8
  1.9 0.0 copy-start.6
  1.9 0.0 copy-start.7
  1.9 0.0 copy-start.9
  1.9 0.0 copy-start.10
  1.9 0.0 copy-start.11
  1.9 7.9 %tree_of_maps.1 = (bf16[31,128,256]{2,1,0:T(8,128)(2,1)S(1)}, bf16[31,128,256]{2,1,0:T(8,128)(2,1)S(1)}, bf16[16,128,256]{2,1,0:T(8,128)(2,1)S(1)}, f32[4,128,128]{2,1,0:T(8,128)}) custom-call(s32[64]{0:T(128)S(1)} %copy-done.8, f32[16,128,128]{2,1,0:T(8,128)S(1)} %copy-done.2), custom_call_target="tpu_custom_call" | custom-call | tf_op jit(solution)/shard_map/tree_of_maps/pallas_call | solution.py:244
  9.8 0.0 copy-start
  9.8 1.3 %copy-done = bf16[31,128,256]{2,1,0:T(8,128)(2,1)} copy-done((bf16[31,128,256]{2,1,0:T(8,128)(2,1)}, bf16[31,128,256]{2,1,0:T(8,128)(2,1)S(1)}, u32[]{:S(2)}) %copy-start) | copy-done | bytes 2031640
  11.1 4.2 %all-to-all-start.1 = ((f32[4,128,128]{2,1,0:T(8,128)}), f32[4,128,128]{2,1,0:T(8,128)S(1)}, u32[]{:S(2)}, u32[]{:S(2)}) async-start(f32[4,128,128]{2,1,0:T(8,128)} %get-tuple-element.15.total_ref), calls=%async_computation.1 | async-start | bytes 524288 | tf_op jit(solution)/shard_map/all_to_all | solution.py:265
  15.3 0.0 copy-start.4
  15.3 0.9 %copy-done.4 = bf16[128,1024]{1,0:T(8,128)(2,1)S(1)} copy-done((bf16[128,1024]{1,0:T(8,128)(2,1)S(1)}, bf16[128,1024]{1,0:T(8,128)(2,1)}, u32[]{:S(2)}) %copy-start.4) | copy-done | bytes 262168
  16.3 0.1 turn_frames.1
  16.4 0.0 copy-start.3
  16.4 0.7 %copy-done.3 = bf16[1024,128]{1,0:T(8,128)(2,1)} copy-done((bf16[1024,128]{1,0:T(8,128)(2,1)}, bf16[1024,128]{1,0:T(8,128)(2,1)S(1)}, u32[]{:S(2)}) %copy-start.3) | copy-done | bytes 262168
  17.1 4.3 %all-to-all-done.1.maps_ref.members_ref = f32[4,128,128]{2,1,0:T(8,128)S(1)} async-done(((f32[4,128,128]{2,1,0:T(8,128)}), f32[4,128,128]{2,1,0:T(8,128)S(1)}, u32[]{:S(2)}, u32[]{:S(2)}) %all-to-all-start.1) | async-done | bytes 262176 | tf_op jit(solution)/shard_map/all_to_all | solution.py:265
  21.4 5.7 %all-to-all-start = ((bf16[16,64,128]{2,1,0:T(8,128)(2,1)}), bf16[16,64,128]{2,1,0:T(8,128)(2,1)}, u32[]{:S(2)}, u32[]{:S(2)}) async-start(bf16[16,64,128]{2,1,0:T(8,128)(2,1)} %bitcast.5), calls=%async_computation | async-start | bytes 524288 | tf_op jit(solution)/shard_map/all_to_all | solution.py:238
  27.0 0.6 group_maps.1
  27.6 0.0 copy-start.5
  27.7 0.7 %copy-done.5 = f32[4,128,128]{2,1,0:T(8,128)} copy-done((f32[4,128,128]{2,1,0:T(8,128)}, f32[4,128,128]{2,1,0:T(8,128)S(1)}, u32[]{:S(2)}) %copy-start.5) | copy-done | bytes 262168
  28.4 8.8 %all-to-all-done.x_ref = bf16[16,64,128]{2,1,0:T(8,128)(2,1)} async-done(((bf16[16,64,128]{2,1,0:T(8,128)(2,1)}), bf16[16,64,128]{2,1,0:T(8,128)(2,1)}, u32[]{:S(2)}, u32[]{:S(2)}) %all-to-all-start) | async-done | bytes 262176 | tf_op jit(solution)/shard_map/all_to_all | solution.py:238
  37.1 12.5 %all_to_all.20.wholes_ref = f32[4,128,128]{2,1,0:T(8,128)S(1)} all-to-all(f32[4,128,128]{2,1,0:T(8,128)} %copy-done.5), channel_id=1, replica_groups={{0,4,8,12},{1,5,9,13},{2,6,10,14},{3,7,11,15},{16,20,24,28},{17,21,25,2..., dimensions={0} | all-to-all | bytes 524288 | tf_op jit(solution)/shard_map/all_to_all | solution.py:274
  49.7 0.0 copy-done.6
  49.7 0.0 copy-done.7
  49.7 0.0 copy-done.9
  49.7 0.0 copy-done.10
  49.7 0.0 copy-done.11
  49.7 0.0 copy-start.1
  49.7 1.6 %copy-done.1 = bf16[31,128,256]{2,1,0:T(8,128)(2,1)S(1)} copy-done((bf16[31,128,256]{2,1,0:T(8,128)(2,1)S(1)}, bf16[31,128,256]{2,1,0:T(8,128)(2,1)}, u32[]{:S(2)}) %copy-start.1) | copy-done | bytes 2031640
  51.3 3.6 %local_states.1 = (f32[64,128]{1,0:T(8,128)S(1)}, f32[16,8,128]{2,1,0:T(8,128)S(1)}) custom-call(s32[1]{0:T(128)} %bitcast.pos_ref, s32[64]{0:T(128)S(1)} %copy-done.9, bf16[16,64,128]{2,1,0:T(8,128)(2,1)} %all-to-all-done.x_ref, s32[16,128]{1,0:T(8,128)S(1)} %bitcast.6, bf16[16,128]{1,0:T(8,128)(2,1)S(1)} %bitcast.7, bf16[128,128]{1,0:T(8,128)(2,1)S(1)} %copy-done.6, ...), custom_call_target="tpu_custom_call" | custom-call | tf_op jit(solution)/shard_map/local_states/pallas_call | solution.py:276
  54.9 9.6 %all_to_all.21.got_ref = f32[16,8,128]{2,1,0:T(8,128)S(1)} all-to-all(f32[16,8,128]{2,1,0:T(8,128)S(1)} %get-tuple-element.17), channel_id=1, replica_groups=mesh['parts'=2,'tm'=16] {'tm'}, dimensions={0} | all-to-all | bytes 131072 | tf_op jit(solution)/shard_map/all_to_all | solution.py:285
  64.5 2.6 %estimates.1 = f32[64,128]{1,0:T(8,128)} custom-call(s32[1]{0:T(128)} %bitcast.pos_ref, s32[64]{0:T(128)S(1)} %copy-done.9, f32[16,8,128]{2,1,0:T(8,128)S(1)} %all_to_all.21.got_ref, f32[1,128]{1,0:T(1,128)S(1)} %bitcast.9, bf16[128,256]{1,0:T(8,128)(2,1)S(1)} %get-tuple-element.18.prefix_ref, bf16[16,128,256]{2,1,0:T(8,128)(2,1)S(1)} %get-tuple-element.13.table_ref, ...), custom_call_target="tpu_custom_call" | custom-call | tf_op jit(solution)/shard_map/estimates/pallas_call | solution.py:286
Async XLA Ops:
  0.0 1.2 %copy-start.2 = (f32[16,128,128]{2,1,0:T(8,128)S(1)}, f32[16,128,128]{2,1,0:T(8,128)}, u32[]{:S(2)}) copy-start(f32[16,128,128]{2,1,0:T(8,128)} %trans_ref.1) | copy-start | bytes 3145732
  1.2 0.7 copy-start.8
  1.9 47.8 %copy-start.6 = (bf16[128,128]{1,0:T(8,128)(2,1)S(1)}, bf16[128,128]{1,0:T(8,128)(2,1)}, u32[]{:S(2)}) copy-start(bf16[128,128]{1,0:T(8,128)(2,1)} %gain_ref.1) | copy-start | bytes 98308
  1.9 47.8 %copy-start.7 = (s32[2048]{0:T(1024)S(1)}, s32[2048]{0:T(1024)}, u32[]{:S(2)}) copy-start(s32[2048]{0:T(1024)} %param.12) | copy-start | bytes 24580
  1.9 47.8 %copy-start.9 = (s32[64]{0:T(128)S(1)}, s32[64]{0:T(128)}, u32[]{:S(2)}) copy-start(s32[64]{0:T(128)} %levels_ref.5) | copy-start | bytes 772
  1.9 47.8 %copy-start.10 = (bf16[2048]{0:T(1024)(128)(2,1)S(1)}, bf16[2048]{0:T(1024)(128)(2,1)}, u32[]{:S(2)}) copy-start(bf16[2048]{0:T(1024)(128)(2,1)} %param.13) | copy-start | bytes 12292
  1.9 47.8 %copy-start.11 = (f32[128]{0:T(128)S(1)}, f32[128]{0:T(128)}, u32[]{:S(2)}) copy-start(f32[128]{0:T(128)} %param.9) | copy-start | bytes 1540
  9.8 1.3 %copy-start = (bf16[31,128,256]{2,1,0:T(8,128)(2,1)}, bf16[31,128,256]{2,1,0:T(8,128)(2,1)S(1)}, u32[]{:S(2)}) copy-start(bf16[31,128,256]{2,1,0:T(8,128)(2,1)S(1)} %get-tuple-element.14.right_ref) | copy-start | bytes 6094852
  11.1 10.2 %all-to-all-start.1 = ((f32[4,128,128]{2,1,0:T(8,128)}), f32[4,128,128]{2,1,0:T(8,128)S(1)}, u32[]{:S(2)}, u32[]{:S(2)}) async-start(f32[4,128,128]{2,1,0:T(8,128)} %get-tuple-element.15.total_ref), calls=%async_computation.1 | async-start | bytes 524288 | tf_op jit(solution)/shard_map/all_to_all | solution.py:265
  15.3 0.9 %copy-start.4 = (bf16[128,1024]{1,0:T(8,128)(2,1)S(1)}, bf16[128,1024]{1,0:T(8,128)(2,1)}, u32[]{:S(2)}) copy-start(bf16[128,1024]{1,0:T(8,128)(2,1)} %frames_ref.1) | copy-start | bytes 786436
  16.4 0.7 %copy-start.3 = (bf16[1024,128]{1,0:T(8,128)(2,1)}, bf16[1024,128]{1,0:T(8,128)(2,1)S(1)}, u32[]{:S(2)}) copy-start(bf16[1024,128]{1,0:T(8,128)(2,1)S(1)} %turn_frames.1) | copy-start | bytes 786436
  21.4 15.8 %all-to-all-start = ((bf16[16,64,128]{2,1,0:T(8,128)(2,1)}), bf16[16,64,128]{2,1,0:T(8,128)(2,1)}, u32[]{:S(2)}, u32[]{:S(2)}) async-start(bf16[16,64,128]{2,1,0:T(8,128)(2,1)} %bitcast.5), calls=%async_computation | async-start | bytes 524288 | tf_op jit(solution)/shard_map/all_to_all | solution.py:238
  27.6 0.7 %copy-start.5 = (f32[4,128,128]{2,1,0:T(8,128)}, f32[4,128,128]{2,1,0:T(8,128)S(1)}, u32[]{:S(2)}) copy-start(f32[4,128,128]{2,1,0:T(8,128)S(1)} %get-tuple-element.16) | copy-start | bytes 786436
  49.7 1.6 %copy-start.1 = (bf16[31,128,256]{2,1,0:T(8,128)(2,1)S(1)}, bf16[31,128,256]{2,1,0:T(8,128)(2,1)}, u32[]{:S(2)}) copy-start(bf16[31,128,256]{2,1,0:T(8,128)(2,1)} %copy-done) | copy-start | bytes 6094852
